TPU v7x, 256 devices: a whole 4x4x8 slice. The times are simulated.
256 devices in a mesh: clus: 128 (over x, z, y), rhs: 2 (over core).
Axes of the slice: x: 4, y: 4, z: 8, core: 2. Of those that a mesh axis runs over, the one named last changes fastest.
Arguments:
- centers: bfloat16 [3, 1048576], P(None, 'clus'), may hold values from -5 to 5
- normals: bfloat16 [3, 1048576], P(None, 'clus'), may hold values from -1 to 1
- weights: bfloat16 [1048576], P('clus'), may hold values from 0.5 to 2
- density: bfloat16 [32, 1048576], P('rhs', 'clus'), may hold values from -6 to 6
- near_pairs: int32 [2, 2, 2048], P(None, None, 'clus'), may hold values from 0 to 15, as said below
- parent: int32 [2048], P('clus'), may hold values from 0 to 7
- far_src: int32 [1024, 32], P('clus'), may hold values from 0 to 1023
- src_basis: bfloat16 [2048, 32, 512], P('clus'), may hold values from -0.25 to 0.25
- upward_transfer: float32 [2048, 32, 32], P('clus'), may hold values from -1 to 1
- far_mat: bfloat16 [1024, 32, 1024], P('clus'), may hold values from -0.1875 to 0.1875
- downward_transfer: float32 [2048, 32, 32], P('clus'), may hold values from -1 to 1
- tgt_basis: bfloat16 [2048, 32, 512], P('clus'), may hold values from -1 to 1
Outputs:
- potential: float32 [32, 1048576], P('rhs', 'clus')
Inputs may be any that keep to these rules, and one draw needn't show every extreme that they name: `near_pairs`: for each device and offset the targets name each of the device's 16 clusters once, and the sources name exactly 8 distinct clusters.
All inputs are finite; a program needn't handle non-finite values.
Results may differ from a plain program's by a relative error of at most 0.0029.
Values may be sent and summed in bfloat16 or wider, within the bound.
A program may use at most 64 MiB of HBM per device.

v0:
```python
import jax
import jax.numpy as jnp
from jax import lax
from jax.sharding import PartitionSpec as P

W = 2


DELTA2 = 0.25
MAX_PRECISION = lax.Precision.HIGHEST


def from_behind(block, axis, distance):
    devices = range(lax.axis_size(axis))
    route = [(i - distance, i) for i in devices if i - distance in devices]
    return lax.ppermute(block, axis, route)


def panel_tiles(tgt_geo, src_geo):
    tgt_geo = tgt_geo.astype(jnp.float32)
    src_geo = src_geo.astype(jnp.float32)
    delta_xyz = tgt_geo[0:3, :, None] - src_geo[0:3, None, :]
    dist_sq = jnp.sum(delta_xyz * delta_xyz, axis=0) + DELTA2
    kernel_scale = tgt_geo[6][:, None] * src_geo[6][None, :] / (dist_sq * jnp.sqrt(dist_sq))
    forward = (jnp.sum(src_geo[3:6][:, None, :] * delta_xyz, axis=0) * kernel_scale).astype(
        jnp.bfloat16
    )
    backward = (-jnp.sum(tgt_geo[3:6][:, :, None] * delta_xyz, axis=0) * kernel_scale).astype(
        jnp.bfloat16
    )
    return (forward, backward)


def index_cluster(array, cluster):
    return lax.dynamic_index_in_dim(array, cluster, 1, keepdims=False)


def add_cluster(running, addend, cluster):
    return lax.dynamic_update_index_in_dim(
        running, index_cluster(running, cluster) + addend, cluster, 1
    )


def cross_pairs(
    running,
    returned,
    targets,
    slots,
    geometry,
    columns,
    other_geo,
    other_cols,
    first_slot,
    per_core,
):

    def pair_step(slot_idx, carry):
        own_sum, back_sum = carry
        tgt_idx = targets[first_slot + slot_idx]
        src_idx = slots[first_slot + slot_idx]
        forward, backward = panel_tiles(
            index_cluster(geometry, tgt_idx), index_cluster(other_geo, src_idx)
        )
        to_target = jnp.dot(
            index_cluster(other_cols, src_idx), forward.T, preferred_element_type=jnp.float32
        )
        to_source = jnp.dot(
            index_cluster(columns, tgt_idx), backward, preferred_element_type=jnp.float32
        )
        return (add_cluster(own_sum, to_target, tgt_idx), add_cluster(back_sum, to_source, src_idx))

    return lax.fori_loop(0, per_core, pair_step, (running, returned))


def local(
    centers,
    normals,
    weights,
    density,
    near_pairs,
    parent,
    far_src,
    src_basis,
    upward_transfer,
    far_mat,
    downward_transfer,
    tgt_basis,
):
    clusters, rank_dim, panels = src_basis.shape
    half_cols = density.shape[0]
    geometry = jnp.concatenate([centers, normals, weights[None, :]], axis=0).reshape(
        7, clusters, panels
    )
    own_cols = density.reshape(half_cols, clusters, panels)
    columns = lax.all_gather(density, "rhs", axis=0, tiled=True).reshape(-1, clusters, panels)
    per_core = clusters // lax.axis_size("rhs")
    first_slot = lax.axis_index("rhs") * per_core
    all_cols = columns.shape[0]
    running = jnp.zeros((all_cols, clusters, panels), jnp.float32)

    def self_block(slot_idx, running):
        cluster = first_slot + slot_idx
        tgt_geo = index_cluster(geometry, cluster)
        forward, unused = panel_tiles(tgt_geo, tgt_geo)
        addend = jnp.dot(
            index_cluster(columns, cluster), forward.T, preferred_element_type=jnp.float32
        )
        return add_cluster(running, addend, cluster)

    running = lax.fori_loop(0, per_core, self_block, running)
    for offset in range(1, W + 1):
        targets = near_pairs[0, offset - 1]
        sources = near_pairs[1, offset - 1]
        other_geo, other_cols = from_behind((geometry, columns), "clus", -offset)
        returned = jnp.zeros((all_cols, clusters, panels), jnp.float32)
        running, returned = cross_pairs(
            running,
            returned,
            targets,
            sources,
            geometry,
            columns,
            other_geo,
            other_cols,
            first_slot,
            per_core,
        )
        running = running + from_behind(returned, "clus", offset)
    near_part = lax.psum_scatter(
        running.reshape(all_cols, clusters * panels), "rhs", scatter_dimension=0, tiled=True
    )
    leaf_coefficient = jnp.einsum(
        "crp,ncp->crn", src_basis, own_cols, preferred_element_type=jnp.float32
    )
    child_coefficient = jnp.einsum(
        "ypk,ykg->ypg", upward_transfer, leaf_coefficient, precision=MAX_PRECISION
    )
    top_count = far_src.shape[0]
    parent_table = (parent[None, :] == jnp.arange(top_count, dtype=jnp.int32)[:, None]).astype(
        jnp.float32
    )
    top_coef = jnp.einsum("tc,can->tan", parent_table, child_coefficient, precision=MAX_PRECISION)
    all_top = lax.all_gather(top_coef, "clus", axis=0, tiled=True)
    far_count = far_src.shape[1]
    picked = jnp.take(all_top, far_src.reshape(-1), axis=0).reshape(
        top_count, far_count * rank_dim, half_cols
    )
    distant_coefficient = jnp.einsum(
        "tak,tkn->tan", far_mat.astype(jnp.float32), picked, precision=MAX_PRECISION
    )
    downward_coefficient = jnp.einsum(
        "ypk,ykg->ypg",
        downward_transfer,
        jnp.take(distant_coefficient, parent, axis=0),
        precision=MAX_PRECISION,
    ).astype(jnp.bfloat16)
    far_part = jnp.einsum(
        "cap,can->ncp", tgt_basis, downward_coefficient, preferred_element_type=jnp.float32
    )
    return near_part + far_part.reshape(half_cols, clusters * panels)


def solution(mesh):
    placed = (
        P(None, "clus"),
        P(None, "clus"),
        P("clus"),
        P("rhs", "clus"),
        P(None, None, "clus"),
        P("clus"),
        P("clus", None),
        P("clus", None, None),
        P("clus", None, None),
        P("clus", None, None),
        P("clus", None, None),
        P("clus", None, None),
    )
    return jax.shard_map(
        local, mesh=mesh, in_specs=placed, out_specs=P("rhs", "clus"), check_vma=False
    )
```

profile of v0, /device:TPU:28, one launch (start us, length us, event | category | flops | bytes accessed | tf_op | source)
XLA Modules:
  0.0 339.4 jit_solution(50905063704536418)
XLA Ops:
  8.2 1.6 pad_maximum_fusion
  9.8 2.6 collective-permute-start.1
  12.4 2.4 all_gather.6
  15.0 2.4 collective-permute-start
  17.6 17.1 %while.43 = (s32[]{:T(128)}, f32[32,16,512]{2,0,1:T(8,128)S(1)}, s32[]{:T(128)}, bf16[32,16,512]{2,0,1:T(8,128)(2,1)S(1)}, bf16[7,16,512]{2,0,1:T(8,128)(2,1)}, /*index=5*/s32[]{:T(128)}, s32[]{:T(128)}, s32[]{:T(128)}) while((s32[]{:T(128)}, f32[32,16,512]{2,0,1:T(8,128)S(1)}, s32[]{:T(128)}, bf16[32,16,512]{2,0,1:T(8,128)(2,1)S(1)}, ...), condition=%wide.region_3.4_spmd, body=%wide.region_0.3_spmd.sunk | while | flops 21777924 | bytes 4556947 | solution.py:110
  36.5 85.5 %while.44 = (s32[]{:T(128)}, f32[32,16,512]{2,0,1:T(8,128)S(1)}, f32[32,16,512]{2,0,1:T(8,128)S(1)}, s32[]{:T(128)}, s32[16]{0:T(128)}, /*index=5*/s32[16]{0:T(1...) while((s32[]{:T(128)}, f32[32,16,512]{2,0,1:T(8,128)S(1)}, ...), condition=%wide.region_8.9_spmd, body=%wide.region_4.8_spmd.sunk | while | flops 41720844 | bytes 8063279 | solution.py:72
  36.5 1.2 dynamic_slice.188
  44.1 1.6 fusion.85
  45.7 1.5 fusion.86
  54.8 1.6 fusion.85
  56.4 1.5 fusion.86
  65.5 1.6 fusion.85
  67.1 1.5 fusion.86
  68.6 1.2 dynamic_slice.188
  76.2 1.6 fusion.85
  77.8 1.5 fusion.86
  86.9 1.6 fusion.85
  88.5 1.5 fusion.86
  97.6 1.6 fusion.85
  99.1 1.5 fusion.86
  108.2 1.6 fusion.85
  109.8 1.5 fusion.86
  118.9 1.6 fusion.85
  120.5 1.5 fusion.86
  122.0 5.6 %collective-permute-start.2 = (f32[32,16,512]{2,0,1:T(8,128)S(1)}, f32[32,16,512]{2,0,1:T(8,128)}, u32[]{:S(2)}, u32[]{:S(2)}) collective-permute-start(f32[32,16,512]{2,0,1:T(8,128)S(1)} %get-tuple-element.441), channel_id=1, source_target_pairs={{0,2},{2,4},{4,6},{6,8},{8,10},{10,12},{12,14},{14,16},{16,18},{18... | collective-permute-start | bytes 3145736 | tf_op jit(solution)/shard_map/ppermute | solution.py:16
  127.6 7.0 %collective-permute-start.4 = (bf16[7,16,512]{2,0,1:T(8,128)(2,1)}, bf16[7,16,512]{2,0,1:T(8,128)(2,1)S(1)}, u32[]{:S(2)}, u32[]{:S(2)}) collective-permute-start(bf16[7,16,512]{2,0,1:T(8,128)(2,1)} %pad_maximum_fusion), channel_id=1, source_target_pairs={{4,0},{6,2},{8,4},{10,6},{12,8},{14,10},{16,12},{18,14},{20,16},{2... | collective-permute-start | bytes 344072 | tf_op jit(solution)/shard_map/ppermute | solution.py:16
  134.6 7.7 %collective-permute-start.3 = (bf16[32,16,512]{2,1,0:T(8,128)(2,1)}, bf16[32,16,512]{2,1,0:T(8,128)(2,1)}, u32[]{:S(2)}, u32[]{:S(2)}) collective-permute-start(bf16[32,16,512]{2,1,0:T(8,128)(2,1)} %bitcast.183), channel_id=1, source_target_pairs={{4,0},{6,2},{8,4},{10,6},{12,8},{14,10},{16,12},{18,14},{20,16},{2... | collective-permute-start | bytes 1572872 | tf_op jit(solution)/shard_map/ppermute | solution.py:16
  142.6 1.5 convolution_bitcast_fusion.1
  145.0 8.3 %collective-permute-done.3 = bf16[32,16,512]{2,1,0:T(8,128)(2,1)} collective-permute-done((bf16[32,16,512]{2,1,0:T(8,128)(2,1)}, bf16[32,16,512]{2,1,0:T(8,128)(2,1)}, u32[]{:S(2)}, u32[]{:S(2)}) %collective-permute-start.3) | collective-permute-done | bytes 524320 | tf_op jit(solution)/shard_map/ppermute | solution.py:16
  153.3 1.3 copy.46
  154.6 1.4 add.234
  156.2 71.4 %while.45 = (s32[]{:T(128)}, f32[32,16,512]{2,0,1:T(8,128)S(1)}, f32[32,16,512]{2,0,1:T(8,128)S(1)}, s32[]{:T(128)}, s32[16]{0:T(128)S(1)}, /*index=5*/s32[16]{0...) while((s32[]{:T(128)}, f32[32,16,512]{2,0,1:T(8,128)S(1)}, ...), condition=%wide.region_13.14_spmd, body=%wide.region_9.13_spmd.sunk | while | flops 41720844 | bytes 8063279 | solution.py:72
  163.6 1.5 fusion.91
  172.6 1.5 fusion.91
  181.5 1.5 fusion.91
  190.4 1.5 fusion.91
  199.4 1.5 fusion.91
  208.3 1.5 fusion.91
  217.2 1.5 fusion.91
  226.2 1.5 fusion.91
  227.6 15.2 %collective-permute-start.5 = (f32[32,16,512]{2,0,1:T(8,128)S(1)}, f32[32,16,512]{2,0,1:T(8,128)S(1)}, u32[]{:S(2)}, u32[]{:S(2)}) collective-permute-start(f32[32,16,512]{2,0,1:T(8,128)S(1)} %get-tuple-element.443), channel_id=1, source_target_pairs={{0,4},{2,6},{4,8},{6,10},{8,12},{10,14},{12,16},{14,18},{16,20},{1... | collective-permute-start | bytes 3145736 | tf_op jit(solution)/shard_map/ppermute | solution.py:16
  242.8 37.8 %collective-permute-done.5 = f32[32,16,512]{2,0,1:T(8,128)S(1)} collective-permute-done((f32[32,16,512]{2,0,1:T(8,128)S(1)}, f32[32,16,512]{2,0,1:T(8,128)S(1)}, u32[]{:S(2)}, u32[]{:S(2)}) %collective-permute-start.5) | collective-permute-done | bytes 1048608 | tf_op jit(solution)/shard_map/ppermute | solution.py:16
  282.4 25.3 %all-gather.2.cloned.1.call-done = f32[1024,32,16]{1,0,2:T(8,128)} async-done(((f32[8,32,16]{1,0,2:T(8,128)}), f32[1024,32,16]{1,0,2:T(8,128)}) %all-gather.2.cloned.1.call-update) | async-done | bytes 2097168 | tf_op jit(solution)/shard_map/all_gather | solution.py:143
  307.6 11.5 %copy.51 = f32[1024,32,16]{1,2,0:T(8,128)} copy(f32[1024,32,16]{1,0,2:T(8,128)} %all-gather.2.cloned.1.call-done) | data formatting | bytes 4194304 | tf_op jit(solution)/shard_map/all_gather | solution.py:143
  319.1 4.1 %gather_fusion = f32[256,32,16]{1,2,0:T(8,128)S(1)} fusion(f32[1024,32,16]{1,2,0:T(8,128)} %copy.51, s32[1024]{0:T(1024)S(1)} %pad_clamp_fusion.1), kind=kCustom, calls=%fused_computation | custom fusion | bytes 1049600 | tf_op jit(solution)/shard_map/jit(_take)/gather | solution.py:145
  323.2 2.0 copy.52
  325.2 2.5 gather.11
  330.0 1.9 add.241
  (254 shorter events, 83.8 us)
Async XLA Ops:
  7.4 322.4 %copy-start = (bf16[16,32,512]{2,1,0:T(8,128)(2,1)S(1)}, bf16[16,32,512]{2,1,0:T(8,128)(2,1)}, u32[]{:S(2)}) copy-start(bf16[16,32,512]{2,1,0:T(8,128)(2,1)} %param.29) | copy-start | bytes 1572868
  7.4 300.2 %all-gather.2.cloned.1.call-start = ((), (), s32[]{:S(2)}) async-start(), calls=%async_computation.2 | async-start | bytes 8454144 | tf_op jit(solution)/shard_map/all_gather | solution.py:143
  9.8 26.5 %collective-permute-start.1 = (bf16[7,16,512]{2,0,1:T(8,128)(2,1)}, bf16[7,16,512]{2,0,1:T(8,128)(2,1)S(1)}, u32[]{:S(2)}, u32[]{:S(2)}) collective-permute-start(bf16[7,16,512]{2,0,1:T(8,128)(2,1)} %pad_maximum_fusion), channel_id=1, source_target_pairs={{2,0},{4,2},{6,4},{8,6},{10,8},{12,10},{14,12},{16,14},{18,16},{20... | collective-permute-start | bytes 344072 | tf_op jit(solution)/shard_map/ppermute | solution.py:16
  15.0 2.6 copy-start.5
  15.0 20.2 %collective-permute-start = (bf16[32,16,512]{2,1,0:T(8,128)(2,1)S(1)}, bf16[32,16,512]{2,1,0:T(8,128)(2,1)S(1)}, u32[]{:S(2)}, u32[]{:S(2)}) collective-permute-start(bf16[32,16,512]{2,1,0:T(8,128)(2,1)S(1)} %bitcast.182), channel_id=1, source_target_pairs={{2,0},{4,2},{6,4},{8,6},{10,8},{12,10},{14,12},{16,14},{18,16},{20... | collective-permute-start | bytes 1572872 | tf_op jit(solution)/shard_map/ppermute | solution.py:16
  17.5 17.1 %copy-start.8 = (s32[2,2,16]{2,1,0:T(2,128)S(1)}, s32[2,2,16]{2,1,0:T(2,128)}, u32[]{:S(2)}) copy-start(s32[2,2,16]{2,1,0:T(2,128)} %param.22) | copy-start | bytes 772
  34.7 1.6 copy-start.4
  36.4 105.9 %copy-start.1 = (bf16[16,8192]{1,0:T(8,128)(2,1)S(1)}, bf16[16,8192]{1,0:T(8,128)(2,1)}, u32[]{:S(2)}) copy-start(bf16[16,8192]{1,0:T(8,128)(2,1)} %param.21) | copy-start | bytes 786436
  36.5 105.9 %copy-start.2 = (bf16[16,32,512]{2,1,0:T(8,128)(2,1)S(1)}, bf16[16,32,512]{2,1,0:T(8,128)(2,1)}, u32[]{:S(2)}) copy-start(bf16[16,32,512]{2,1,0:T(8,128)(2,1)} %param.25) | copy-start | bytes 1572868
  36.5 107.6 %copy-start.9 = (s32[16]{0:T(128)S(1)}, s32[16]{0:T(128)}, u32[]{:S(2)}) copy-start(s32[16]{0:T(128)} %param.23) | copy-start | bytes 196
  122.0 32.6 %collective-permute-start.2 = (f32[32,16,512]{2,0,1:T(8,128)S(1)}, f32[32,16,512]{2,0,1:T(8,128)}, u32[]{:S(2)}, u32[]{:S(2)}) collective-permute-start(f32[32,16,512]{2,0,1:T(8,128)S(1)} %get-tuple-element.441), channel_id=1, source_target_pairs={{0,2},{2,4},{4,6},{6,8},{8,10},{10,12},{12,14},{14,16},{16,18},{18... | collective-permute-start | bytes 3145736 | tf_op jit(solution)/shard_map/ppermute | solution.py:16
  127.6 28.5 %collective-permute-start.4 = (bf16[7,16,512]{2,0,1:T(8,128)(2,1)}, bf16[7,16,512]{2,0,1:T(8,128)(2,1)S(1)}, u32[]{:S(2)}, u32[]{:S(2)}) collective-permute-start(bf16[7,16,512]{2,0,1:T(8,128)(2,1)} %pad_maximum_fusion), channel_id=1, source_target_pairs={{4,0},{6,2},{8,4},{10,6},{12,8},{14,10},{16,12},{18,14},{20,16},{2... | collective-permute-start | bytes 344072 | tf_op jit(solution)/shard_map/ppermute | solution.py:16
  134.6 18.7 %collective-permute-start.3 = (bf16[32,16,512]{2,1,0:T(8,128)(2,1)}, bf16[32,16,512]{2,1,0:T(8,128)(2,1)}, u32[]{:S(2)}, u32[]{:S(2)}) collective-permute-start(bf16[32,16,512]{2,1,0:T(8,128)(2,1)} %bitcast.183), channel_id=1, source_target_pairs={{4,0},{6,2},{8,4},{10,6},{12,8},{14,10},{16,12},{18,14},{20,16},{2... | collective-permute-start | bytes 1572872 | tf_op jit(solution)/shard_map/ppermute | solution.py:16
  145.0 185.1 %reduce-scatter.2.cloned.1.call-start = ((), (), s32[]{:S(2)}) async-start(), calls=%async_computation.1 | async-start | bytes 1572864 | tf_op jit(solution)/shard_map/reduce_scatter | solution.py:129
  227.6 53.0 %collective-permute-start.5 = (f32[32,16,512]{2,0,1:T(8,128)S(1)}, f32[32,16,512]{2,0,1:T(8,128)S(1)}, u32[]{:S(2)}, u32[]{:S(2)}) collective-permute-start(f32[32,16,512]{2,0,1:T(8,128)S(1)} %get-tuple-element.443), channel_id=1, source_target_pairs={{0,4},{2,6},{4,8},{6,10},{8,12},{10,14},{12,16},{14,18},{16,20},{1... | collective-permute-start | bytes 3145736 | tf_op jit(solution)/shard_map/ppermute | solution.py:16
  280.6 1.3 copy-start.7
  323.2 4.5 %copy-start.3 = (bf16[8,32,1024]{2,1,0:T(8,128)(2,1)S(1)}, bf16[8,32,1024]{2,1,0:T(8,128)(2,1)}, u32[]{:S(2)}) copy-start(bf16[8,32,1024]{2,1,0:T(8,128)(2,1)} %param.27) | copy-start | bytes 1572868
  325.2 3.9 %copy-start.6 = (f32[16,32,32]{2,1,0:T(8,128)S(1)}, f32[16,32,32]{2,1,0:T(8,128)}, u32[]{:S(2)}) copy-start(f32[16,32,32]{2,1,0:T(8,128)} %param.28) | copy-start | bytes 196612
Sparse Core Ops, SparseCore 0:
  145.1 162.4 all-gather.1
Sparse Core Ops, SparseCore 1:
  282.0 24.1 reduce-scatter.1
where the time goes:
time: 343 us; the launch traced here: 339 us
  waiting for transfers between devices  71.4 us (21%)
  loops' own time  59.6 us (17%)
  matrix products  53.6 us (16%)
  local copies, waits for them, and re-layouts  51.1 us (15%)
  other arithmetic  45.5 us (13%)
  starting transfers between devices  40.5 us (12%)
  between operations  15.2 us (4%)
    another operation x2, loops' own time, cross_pairs(): return lax.fori_loop(0, per_core, pair_step, (running, returned))  59.3 us
    ppermute x6, waiting for transfers between devices, from_behind(): return lax.ppermute(block, axis, route)  46.1 us
    ppermute x6, starting transfers between devices, from_behind(): return lax.ppermute(block, axis, route)  40.5 us
    all_gather x1, waiting for transfers between devices, local(): all_top = lax.all_gather(top_coef, 'clus', axis=0, tiled=True)  25.3 us
    dot_general x16, matrix products, pair_step(): jnp.dot(index_cluster(columns, tgt_idx), backward, preferred_element_type...  23.7 us
    dot_general x16, matrix products, pair_step(): jnp.dot(index_cluster(other_cols, src_idx), forward.T, preferred_element_...  19.3 us
    reduce_sum x16, other arithmetic, panel_tiles(): jnp.sum(tgt_geo[3:6][:, :, None] * delta_xyz, axis=0)  18.8 us
    dynamic_slice x16, local copies, waits for them, and re-layouts, pair_step(): tgt_idx = targets[first_slot + slot_idx]  14.2 us
  transfers between devices with their start and end apart: 8, of which 3 were waited for; matrix products, arithmetic and copies ran while one was open for 27% of the time, Pallas kernels for 0%

commit v1 on v0

v1 whole, which is shorter than its diff:
```python
import functools

import jax
import jax.numpy as jnp
from jax import lax
from jax.experimental import pallas as pl
from jax.experimental.pallas import tpu as pltpu
from jax.sharding import PartitionSpec as P

F32 = jnp.float32
BF16 = jnp.bfloat16
MESH = pl.DeviceIdType.MESH
HIGHEST = lax.Precision.HIGHEST

DELTA2 = 0.25
W = 2
X, Z, Y = 4, 8, 4
N = X * Z * Y
CL = 16
HALF = 8
CAP = 8
PS = 512
COLS = 16
RANK = 32
TOPS = 8
FAR = 32

LIST, SLOT, RANKED, PRESENT = 0, 8, 24, 40


def mm(a, b, precision=None):
    return jnp.dot(a, b, preferred_element_type=F32, precision=precision)


def mm_nt(a, b, precision=None):
    return lax.dot_general(
        a, b, (((1,), (1,)), ((), ())), preferred_element_type=F32, precision=precision
    )


def split3(v):
    high = v.astype(BF16).astype(F32)
    rest = v - high
    mid = rest.astype(BF16).astype(F32)
    return high, mid, rest - mid


def features(geo):
    row = lax.broadcasted_iota(jnp.int32, geo.shape, 0)
    low = row < 3
    mid = (row >= 3) & (row < 6)
    w = geo[6:7]
    weighted = geo * w
    xh = weighted.astype(BF16).astype(F32)
    xl = weighted - xh
    yh = jnp.where(low, jnp.roll(xh, -3, axis=0), 0.0)
    yl = jnp.where(low, jnp.roll(xl, -3, axis=0), 0.0)
    c0, c1, c2 = geo[0:1], geo[1:2], geo[2:3]
    square = c0 * c0 + c1 * c1 + c2 * c2 + 0.5 * DELTA2
    offset = -(weighted[3:4] * c0 + weighted[4:5] * c1 + weighted[5:6] * c2)

    def rows_3_to_5(parts, base):
        h, m, l = parts
        return jnp.where(row == 3, h, jnp.where(row == 4, m, jnp.where(row == 5, l, base)))

    sh, sm, sl = split3(square)
    q1 = [
        rows_3_to_5((sh, sm, sl), jnp.where(low, -2.0 * geo, 0.0)),
        jnp.where(low, 1.0, 0.0),
    ]
    q2 = [
        jnp.where(low, geo, jnp.where(mid, 1.0, 0.0)),
        jnp.where(row == 0, sh, jnp.where(row == 1, sm, jnp.where(row == 2, sl, 0.0))),
    ]
    u = [jnp.where(low, xh, jnp.where(mid, w, 0.0)), xl, xh, xl]
    v = [rows_3_to_5(split3(offset), yh), yh, yl, yl]
    return q1, q2, u, v


def target_features(geo):
    q1, q2, u, v = features(geo)
    pad = jnp.zeros((48, PS), F32)
    left = jnp.concatenate(q1 + u + v + [pad], axis=0).T.astype(BF16)
    return left, jnp.concatenate(q2 + v + u, axis=0).astype(BF16)


def source_features(geo):
    q1, q2, u, v = features(geo)
    return jnp.concatenate(q2 + v + u, axis=0).astype(BF16)


def cube(q):
    t = lax.rsqrt(q)
    return t * t * t


def kernel(
    cen, nor, wts, den, idx1, idx2, parent, far_idx, src_basis, up, far_mat, down, tgt_basis,
    out,
    geo, dens, left, right, dsib, sendd, sendg, bown1, bown2, bsib1, bsib2, bgeo1, bgeo2, bright, near, ybuf,
    part_own, part_sib, part_recv, ret_send, ret_recv1, ret_recv2, near_sib, near_recv, table, folded, far_top, ridx1, ridx2,
    s_idx, r_idx, s_sib, r_sib, s_bd, r_bd, s_bg, r_bg, s_fd, r_fd, s_fg, r_fg, s_ps, r_ps,
    s_rt, r_rt, s_nr, r_nr, s_z, r_z, s_y, r_y, s_x, r_x,
):
    me = lax.axis_index("clus")
    core = lax.axis_index("rhs")
    y = lax.rem(me, Y)
    z = lax.rem(me // Y, Z)
    x = me // (Y * Z)
    idx = (idx1, idx2)
    ridx = (ridx1, ridx2)
    bown, bsib, bgeo = (bown1, bown2), (bsib1, bsib2), (bgeo1, bgeo2)
    ret_recv = (ret_recv1, ret_recv2)
    mine = core * HALF
    other = (1 - core) * HALF

    def along(step):
        return {"clus": lax.rem(me + step + N, N)}

    sibling = {"rhs": 1 - core}
    z_peers = [{"clus": (x * Z + lax.rem(z + k, Z)) * Y + y} for k in range(1, Z)]
    y_peers = [{"clus": (x * Z + z) * Y + lax.rem(y + k, Y)} for k in range(1, Y)]
    x_peers = [{"clus": (lax.rem(x + k, X) * Z + z) * Y + y} for k in range(1, X)]

    def remote(src, dst, send, recv, to):
        return pltpu.make_async_remote_copy(
            src_ref=src, dst_ref=dst, send_sem=send, recv_sem=recv, device_id=to, device_id_type=MESH
        )

    barrier = pltpu.get_barrier_semaphore()
    partners = [sibling] + [along(s) for s in (1, 2, -1, -2)] + z_peers + y_peers + x_peers
    for partner in partners:
        pl.semaphore_signal(barrier, inc=1, device_id=partner, device_id_type=MESH)
    pl.semaphore_wait(barrier, len(partners))

    idx_copies = [
        remote(idx[o], ridx[o], s_idx.at[o], r_idx.at[o], along(o + 1)) for o in range(W)
    ]
    for copy in idx_copies:
        copy.start()
    sib_copy = remote(
        den.at[:, pl.ds(pl.multiple_of(other * PS, PS), HALF * PS)], dsib, s_sib, r_sib, sibling
    )
    sib_copy.start()

    for c in range(CL):
        at = pl.ds(c * PS, PS)
        rows = [cen[:, at].astype(F32), nor[:, at].astype(F32), wts[:, at].astype(F32)]
        dens[c] = den[:, at]
        geo[c] = jnp.concatenate(rows + [jnp.zeros((1, PS), F32)], axis=0)

    b_copies = []
    for o in range(W):
        idx_copies[o].wait()
        for m in range(CAP):
            c = ridx[o][LIST + m]
            sendd[o, m] = dens[c]
        for m in range(2):
            c0 = ridx[o][LIST + core * 4 + 2 * m]
            c1 = ridx[o][LIST + core * 4 + 2 * m + 1]
            sendg[o, m] = jnp.concatenate([geo[c0], geo[c1]], axis=0).astype(BF16)
        copies = (
            remote(sendg.at[o], bgeo[o].at[pl.ds(core * 2, 2)], s_bg.at[o], r_bg.at[o], along(-o - 1)),
            remote(sendd.at[o], bown[o], s_bd.at[o], r_bd.at[o], along(-o - 1)),
        )
        for copy in copies:
            copy.start()
        b_copies.append(copies)

    tops = [jnp.zeros((COLS, RANK), F32) for _ in range(TOPS)]
    for c in range(CL):
        leaf = mm_nt(den[:, c * PS : (c + 1) * PS], src_basis[c])
        child = mm_nt(leaf, up[c], HIGHEST)
        for t in range(TOPS):
            tops[t] = tops[t] + jnp.where(parent[c] == t, child, 0.0)
    flat = (x * Y + y) * Z + z
    for h in range(2):
        table[2 * flat + h] = jnp.concatenate(tops[4 * h : 4 * h + 4], axis=1).astype(BF16)

    def gather_step(start, size, peers, send, recv):
        block = table.at[pl.ds(start, size)]
        copies = [
            remote(block, block, send.at[k], recv.at[k], to) for k, to in enumerate(peers)
        ]
        for copy in copies:
            copy.start()
        return copies

    z_copies = gather_step(2 * flat, 2, z_peers, s_z, r_z)

    for t in range(HALF):
        left[t], right[t] = target_features(geo[mine + t])
    sib_copy.wait()
    for copy in z_copies:
        copy.wait()
    y_copies = gather_step((x * Y + y) * Z * 2, Z * 2, y_peers, s_y, r_y)

    def densities(t):
        own = den[:, pl.ds(pl.multiple_of((mine + t) * PS, PS), PS)]
        return jnp.concatenate([own, dsib[:, pl.ds(pl.multiple_of(t * PS, PS), PS)]], axis=0)

    def self_pair(u, carry):
        for k in range(2):
            t = 2 * u + k
            q = mm(left[t, :, 0:16], right[t, 0:16])
            nb = mm(left[t, :, 48:80], right[t, 48:80])
            near[t] = mm(densities(t), (nb * cube(q)).astype(BF16))
        return carry

    lax.fori_loop(0, HALF // 2, self_pair, 0)

    for copy in y_copies:
        copy.wait()
    x_copies = gather_step(x * Y * Z * 2, Y * Z * 2, x_peers, s_x, r_x)

    def arrived(o):
        for copy in b_copies[o]:
            copy.wait()
        half = pl.ds(core * 2, 2)
        forwards = (
            remote(bgeo[o].at[half], bgeo[o].at[half], s_fg.at[o], r_fg.at[o], sibling),
            remote(bown[o], bsib[o], s_fd.at[o], r_fd.at[o], sibling),
        )
        for copy in forwards:
            copy.start()
        return forwards

    def cross(o, forwards):
        for copy in forwards:
            copy.wait()
        for m in range(CAP):
            pair = bgeo[o][m // 2].astype(F32)
            bright[m] = source_features(pair[8 * (m % 2) : 8 * (m % 2) + 8])
        live = jnp.where(me + o + 1 < N, 1.0, 0.0).astype(F32)

        def cross_pair(u, carry):
            for k in range(2):
                t = 2 * u + k
                m = idx[o][SLOT + mine + t]
                q = mm(left[t, :, 0:16], bright[m, 0:16])
                nf = mm(left[t, :, 16:48], bright[m, 16:48])
                nb = mm(left[t, :, 48:80], bright[m, 48:80])
                scale = cube(q)
                there = jnp.concatenate([bown[o][m], bsib[o][m]], axis=0)
                near[t] += live * mm_nt(there, (nf * scale).astype(BF16))
                ybuf[t] = mm(densities(t), (nb * scale).astype(BF16))
            return carry

        lax.fori_loop(0, HALF // 2, cross_pair, 0)
        for rows, dst in ((0, part_own), (COLS, part_sib)):
            for r in range(0, COLS, 8):
                tiles = [ybuf[t, rows + r : rows + r + 8, :] for t in range(HALF)]
                for m in range(CAP):
                    total = None
                    for t in range(HALF):
                        hit = jnp.where(idx[o][SLOT + mine + t] == m, 1.0, 0.0).astype(F32)
                        term = hit * tiles[t]
                        total = term if total is None else total + term
                    dst[o, m, r : r + 8, :] = total
        copy = remote(part_sib.at[o], part_recv.at[o], s_ps.at[o], r_ps.at[o], sibling)
        copy.start()
        return copy

    def send_back(o, copy):
        copy.wait()
        for m in range(CAP):
            ret_send[o, m] = (part_own[o, m] + part_recv[o, m]).astype(BF16)
        back = remote(ret_send.at[o], ret_recv[o], s_rt.at[o], r_rt.at[o], along(o + 1))
        back.start()
        return back

    forwards = arrived(0)
    part = cross(0, forwards)
    forwards = arrived(1)
    backs = [send_back(0, part)]
    part = cross(1, forwards)
    for t in range(HALF):
        near_sib[t] = near[t, COLS:, :]
    near_copy = remote(near_sib, near_recv, s_nr, r_nr, sibling)
    near_copy.start()
    backs.append(send_back(1, part))

    for copy in x_copies:
        copy.wait()
    lane = lax.broadcasted_iota(jnp.int32, (COLS, 128), 1) // RANK
    for t in range(TOPS):
        for f in range(FAR):
            code = far_idx[t * FAR + f]
            tile = table[code >> 2].astype(F32)
            folded[t * FAR + f] = jnp.where(lane == (code & 3), tile, 0.0).astype(BF16)
    ones_row = lax.rem(lax.broadcasted_iota(jnp.int32, (128, 128), 0), RANK)
    ones_col = lax.rem(lax.broadcasted_iota(jnp.int32, (128, 128), 1), RANK)
    spread = jnp.where(ones_row == ones_col, 1.0, 0.0).astype(BF16)
    picked = []
    for t in range(TOPS):
        tiles = folded[t * FAR : (t + 1) * FAR].reshape(FAR * COLS, 128)
        everywhere = mm(tiles, spread)
        groups = []
        for g in range(FAR // 4):
            total = None
            for k in range(4):
                f = 4 * g + k
                term = jnp.where(lane == k, everywhere[f * COLS : (f + 1) * COLS], 0.0)
                total = term if total is None else total + term
            groups.append(total.astype(BF16))
        picked.append(jnp.concatenate(groups, axis=1))
    distant = mm_nt(jnp.concatenate(picked, axis=0), far_mat[...])
    for t in range(TOPS):
        far_top[t] = distant[t * COLS : (t + 1) * COLS, t * RANK : (t + 1) * RANK]
    for c in range(CL):
        lower = mm_nt(far_top[parent[c]], down[c], HIGHEST).astype(BF16)
        out[:, c * PS : (c + 1) * PS] = mm(lower, tgt_basis[c])

    near_copy.wait()
    for t in range(HALF):
        at = pl.ds(pl.multiple_of((mine + t) * PS, PS), PS)
        out[:, at] += near[t, 0:COLS, :]
        at = pl.ds(pl.multiple_of((other + t) * PS, PS), PS)
        out[:, at] += near_recv[t]
    for o in range(W):
        backs[o].wait()
        behind = jnp.where(me - o - 1 >= 0, 1.0, 0.0).astype(F32)
        for c in range(CL):
            at = pl.ds(c * PS, PS)
            given = ret_recv[o][ridx[o][RANKED + c]].astype(F32)
            keep = behind * ridx[o][PRESENT + c].astype(F32)
            out[:, at] += keep * given


def index_table(targets, sources):
    slots = jnp.arange(CL, dtype=jnp.int32)
    present = jnp.any(sources[None, :] == slots[:, None], axis=1).astype(jnp.int32)
    rank = jnp.sum(jnp.where(slots[None, :] < slots[:, None], present[None, :], 0), axis=1)
    place = (rank[None, :] == jnp.arange(CAP)[:, None]) & (present[None, :] == 1)
    listed = jnp.sum(jnp.where(place, slots[None, :], 0), axis=1)
    named = jnp.sum(
        jnp.where(targets[None, :] == slots[:, None], sources[None, :], 0), axis=1
    )
    slot = jnp.sum(jnp.where(named[:, None] == slots[None, :], rank[None, :], 0), axis=1)
    rank = jnp.minimum(rank, CAP - 1) * present
    pad = jnp.zeros((128 - 56,), jnp.int32)
    return jnp.concatenate([listed, slot, rank, present, pad]).astype(jnp.int32)


def local(
    centers,
    normals,
    weights,
    density,
    near_pairs,
    parent,
    far_src,
    src_basis,
    upward_transfer,
    far_mat,
    downward_transfer,
    tgt_basis,
):
    tables = [index_table(near_pairs[0, o], near_pairs[1, o]) for o in range(W)]
    dev, lane = far_src // TOPS, far_src % TOPS
    place = ((dev // (Y * Z)) * Y + dev % Y) * Z + (dev // Y) % Z
    far_idx = ((place * 2 + lane // 4) * 4 + lane % 4).reshape(-1).astype(jnp.int32)

    vmem = pl.BlockSpec(memory_space=pltpu.VMEM)
    smem = pl.BlockSpec(memory_space=pltpu.SMEM)
    dma = pltpu.SemaphoreType.DMA
    return pl.pallas_call(
        kernel,
        out_shape=jax.ShapeDtypeStruct((COLS, CL * PS), F32),
        in_specs=[vmem] * 4 + [smem] * 4 + [vmem] * 5,
        out_specs=vmem,
        scratch_shapes=[
            pltpu.VMEM((CL, 8, PS), F32),
            pltpu.VMEM((CL, COLS, PS), BF16),
            pltpu.VMEM((HALF, PS, 128), BF16),
            pltpu.VMEM((HALF, 80, PS), BF16),
            pltpu.VMEM((COLS, HALF * PS), BF16),
            pltpu.VMEM((W, CAP, COLS, PS), BF16),
            pltpu.VMEM((W, 2, 16, PS), BF16),
            pltpu.VMEM((CAP, COLS, PS), BF16),
            pltpu.VMEM((CAP, COLS, PS), BF16),
            pltpu.VMEM((CAP, COLS, PS), BF16),
            pltpu.VMEM((CAP, COLS, PS), BF16),
            pltpu.VMEM((4, 16, PS), BF16),
            pltpu.VMEM((4, 16, PS), BF16),
            pltpu.VMEM((CAP, 80, PS), BF16),
            pltpu.VMEM((HALF, 2 * COLS, PS), F32),
            pltpu.VMEM((HALF, 2 * COLS, PS), F32),
            pltpu.VMEM((W, CAP, COLS, PS), F32),
            pltpu.VMEM((W, CAP, COLS, PS), F32),
            pltpu.VMEM((W, CAP, COLS, PS), F32),
            pltpu.VMEM((W, CAP, COLS, PS), BF16),
            pltpu.VMEM((CAP, COLS, PS), BF16),
            pltpu.VMEM((CAP, COLS, PS), BF16),
            pltpu.VMEM((HALF, COLS, PS), F32),
            pltpu.VMEM((HALF, COLS, PS), F32),
            pltpu.VMEM((2 * N, COLS, 128), BF16),
            pltpu.VMEM((TOPS * FAR, COLS, 128), BF16),
            pltpu.VMEM((TOPS, COLS, RANK), F32),
            pltpu.SMEM((128,), jnp.int32),
            pltpu.SMEM((128,), jnp.int32),
            dma((W,)), dma((W,)),
            dma, dma,
            dma((W,)), dma((W,)),
            dma((W,)), dma((W,)),
            dma((W,)), dma((W,)),
            dma((W,)), dma((W,)),
            dma((W,)), dma((W,)),
            dma((W,)), dma((W,)),
            dma, dma,
            dma((Z - 1,)), dma((Z - 1,)),
            dma((Y - 1,)), dma((Y - 1,)),
            dma((X - 1,)), dma((X - 1,)),
        ],
        compiler_params=pltpu.CompilerParams(
            collective_id=0, has_side_effects=True, vmem_limit_bytes=56 * 1024 * 1024
        ),
    )(
        centers,
        normals,
        weights.reshape(1, -1),
        density,
        *tables,
        parent,
        far_idx,
        src_basis,
        upward_transfer,
        far_mat.reshape(TOPS * RANK, FAR * RANK),
        downward_transfer,
        tgt_basis,
    )


def solution(mesh):
    placed = (
        P(None, "clus"),
        P(None, "clus"),
        P("clus"),
        P("rhs", "clus"),
        P(None, None, "clus"),
        P("clus"),
        P("clus", None),
        P("clus", None, None),
        P("clus", None, None),
        P("clus", None, None),
        P("clus", None, None),
        P("clus", None, None),
    )
    return jax.shard_map(
        local, mesh=mesh, in_specs=placed, out_specs=P("rhs", "clus"), check_vma=False
    )
```

time: 343 us -> 62.8 us (0.18)
  the two profiles are of different devices: /device:TPU:28 before, /device:TPU:1 now
where the time goes in v1:
time: 62.8 us; the launch traced here: 62.6 us
  Pallas kernels  56.2 us (89%)
  local copies, waits for them, and re-layouts  5.21 us (8%)
  other arithmetic  1.11 us (2%)
    pallas_call x1, Pallas kernels, local(): pl.pallas_call(kernel, out_shape=jax.ShapeDtypeStruct((COLS, CL * PS), F3...  56.2 us
    unnamed x5, local copies, waits for them, and re-layouts  1.88 us
    concatenate x2, local copies, waits for them, and re-layouts, index_table(): return jnp.concatenate([listed, slot, rank, present, pad]).astype(jnp.int32)  1.26 us

profile of v1, /device:TPU:1, one launch (start us, length us, event | category | flops | bytes accessed | tf_op | source)
XLA Modules:
  0.0 62.6 jit_solution(12595164531247110341)
XLA Ops:
  0.0 0.8 %slice_bitcast_fusion = (s32[16]{0:T(128)S(1)}, s32[16]{0:T(128)S(1)}, s32[16]{0:T(128)S(1)}, s32[16]{0:T(128)S(1)}) fusion(s32[2,2,16]{2,1,0:T(2,128)} %param.16), kind=kLoop, calls=%fused_computation.63 | loop fusion | bytes 512 | tf_op jit(solution)/shard_map/eq | solution.py:337
  0.8 0.1 select_reduce_fusion.1
  0.9 0.1 fusion
  1.0 0.1 select_reduce_fusion.5
  1.1 0.2 select_reduce_fusion.3
  1.3 0.1 select_reduce_fusion.7
  1.4 0.0 copy-start.1
  1.5 0.0 copy-start
  1.5 0.6 concatenate.6.idx1
  2.1 0.1 select_reduce_fusion.2
  2.2 0.2 select_reduce_fusion
  2.4 0.1 select_reduce_fusion.6
  2.5 0.7 %concatenate.7.idx2 = s32[128]{0:T(128)} concatenate(s32[8]{0:T(128)S(1)} %select_reduce_fusion.6, s32[16]{0:T(128)S(1)} %select_reduce_fusion, s32[16]{0:T(128)S(1)} %minimum_select_fusion, s32[16]{0:T(128)S(1)} %get-tuple-element.10, s32[72]{0:T(128)S(1)} %broadcast.70), dimensions={0} | concatenate | bytes 1024 | tf_op jit(solution)/shard_map/concatenate | solution.py:342
  3.2 0.0 copy-done.1
  3.2 0.7 %reshape.32.far_idx = s32[256]{0:T(256)} reshape(s32[8,32]{1,0:T(8,128)S(1)} %fusion.10) | data formatting | bytes 2048 | tf_op jit(solution)/shard_map/reshape | solution.py:362
  3.9 0.0 copy-done
  3.9 0.6 %reshape.31.wts = bf16[1,8192]{1,0:T(2,128)(2,1)} reshape(bf16[8192]{0:T(1024)(128)(2,1)S(1)} %copy-done) | data formatting | bytes 32768 | tf_op jit(solution)/shard_map/reshape | solution.py:421
  4.5 56.2 %shard_map.118 = f32[16,8192]{1,0:T(8,128)} custom-call(bf16[3,8192]{1,0:T(4,128)(2,1)} %cen.1, bf16[3,8192]{1,0:T(4,128)(2,1)} %nor.1, bf16[1,8192]{1,0:T(2,128)(2,1)} %reshape.31.wts, bf16[16,8192]{1,0:T(8,128)(2,1)} %den.1, s32[128]{0:T(128)} %concatenate.6.idx1, s32[128]{0:T(128)} %concatenate.7.idx2, s32[16]{0:T(128)} %parent.1, s32[256]{0:T(256)} %reshape.32.far_idx, ...), custom_call_target="tpu_custom_call" | custom-call | tf_op jit(solution)/shard_map/pallas_call | solution.py:367
  60.7 1.9 %copy.14 = f32[16,8192]{1,0:T(8,128)} copy(f32[16,8192]{1,0:T(8,128)} %shard_map.118) | data formatting | bytes 1048576
  (6 shorter events, 0.1 us)
Async XLA Ops:
  1.4 1.7 %copy-start.1 = (s32[8,32]{1,0:T(8,128)S(1)}, s32[8,32]{1,0:T(8,128)}, u32[]{:S(2)}) copy-start(s32[8,32]{1,0:T(8,128)} %param.18) | copy-start | bytes 3076
  1.5 2.4 %copy-start = (bf16[8192]{0:T(1024)(128)(2,1)S(1)}, bf16[8192]{0:T(1024)(128)(2,1)}, u32[]{:S(2)}) copy-start(bf16[8192]{0:T(1024)(128)(2,1)} %param.14) | copy-start | bytes 49156

commit v2 on v1

--- a/solution.py
+++ b/solution.py
@@ -25,7 +25,9 @@
 TOPS = 8
 FAR = 32
 
-LIST, SLOT, RANKED, PRESENT = 0, 8, 24, 40
+LIST, RANKED, PRESENT = 0, 8, 24
+POWER, LOG = 0, 16
+PRIME = 19
 
 
 def mm(a, b, precision=None):
@@ -94,11 +96,38 @@
     return t * t * t
 
 
+def name_sources(pairs, o, small, idx):
+    named = 0
+    for p in range(CL):
+        named = named | small[POWER + pairs[1, o, p]]
+    before = 0
+    for c in range(CL):
+        present = (named >> c) & 1
+        idx[RANKED + c] = before * present
+        idx[PRESENT + c] = present
+        before = before + present
+    for m in range(CAP):
+        lowest = named & (-named)
+        idx[LIST + m] = small[LOG + lax.rem(lowest, PRIME)]
+        named = named - lowest
+
+
+def name_targets(pairs, o, mine, idx, slots):
+    for t in range(HALF):
+        source = 0
+        for p in range(CL):
+            source = source + jnp.where(pairs[0, o, p] == mine + t, pairs[1, o, p], 0)
+        slots[t] = idx[RANKED + source]
+
+
 def kernel(
-    cen, nor, wts, den, idx1, idx2, parent, far_idx, src_basis, up, far_mat, down, tgt_basis,
+    cen, nor, wts, den, pairs, parent, far_src, src_basis_hbm, up_hbm, far_mat_hbm, down_hbm,
+    tgt_basis_hbm,
     out,
-    geo, dens, left, right, dsib, sendd, sendg, bown1, bown2, bsib1, bsib2, bgeo1, bgeo2, bright, near, ybuf,
-    part_own, part_sib, part_recv, ret_send, ret_recv1, ret_recv2, near_sib, near_recv, table, folded, far_top, ridx1, ridx2,
+    src_basis, up, far_mat, down, tgt_basis, s_in,
+    small, geo, dens, left, right, dsib, sendd, sendg, bown1, bown2, bsib1, bsib2, bgeo1, bgeo2,
+    bright, near, ybuf, fbuf, part_own, part_sib, part_recv, ret_send, ret_recv1, ret_recv2,
+    near_sib, near_recv, table, folded, far_top, idx1, idx2, ridx1, ridx2, slots1, slots2,
     s_idx, r_idx, s_sib, r_sib, s_bd, r_bd, s_bg, r_bg, s_fd, r_fd, s_fg, r_fg, s_ps, r_ps,
     s_rt, r_rt, s_nr, r_nr, s_z, r_z, s_y, r_y, s_x, r_x,
 ):
@@ -109,6 +138,7 @@
     x = me // (Y * Z)
     idx = (idx1, idx2)
     ridx = (ridx1, ridx2)
+    slots = (slots1, slots2)
     bown, bsib, bgeo = (bown1, bown2), (bsib1, bsib2), (bgeo1, bgeo2)
     ret_recv = (ret_recv1, ret_recv2)
     mine = core * HALF
@@ -131,6 +161,28 @@
     partners = [sibling] + [along(s) for s in (1, 2, -1, -2)] + z_peers + y_peers + x_peers
     for partner in partners:
         pl.semaphore_signal(barrier, inc=1, device_id=partner, device_id_type=MESH)
+    loads = [
+        pltpu.make_async_copy(src, dst, s_in.at[k])
+        for k, (src, dst) in enumerate(
+            (
+                (src_basis_hbm, src_basis),
+                (up_hbm, up),
+                (far_mat_hbm, far_mat),
+                (down_hbm, down),
+                (tgt_basis_hbm, tgt_basis),
+            )
+        )
+    ]
+    for load in loads:
+        load.start()
+    for c in range(CL):
+        small[POWER + c] = 1 << c
+    for p in range(PRIME):
+        small[LOG + p] = 0
+    for c in range(CL):
+        small[LOG + (1 << c) % PRIME] = c
+    for o in range(W):
+        name_sources(pairs, o, small, idx[o])
     pl.semaphore_wait(barrier, len(partners))
 
     idx_copies = [
@@ -149,33 +201,16 @@
         dens[c] = den[:, at]
         geo[c] = jnp.concatenate(rows + [jnp.zeros((1, PS), F32)], axis=0)
 
-    b_copies = []
-    for o in range(W):
-        idx_copies[o].wait()
-        for m in range(CAP):
-            c = ridx[o][LIST + m]
-            sendd[o, m] = dens[c]
-        for m in range(2):
-            c0 = ridx[o][LIST + core * 4 + 2 * m]
-            c1 = ridx[o][LIST + core * 4 + 2 * m + 1]
-            sendg[o, m] = jnp.concatenate([geo[c0], geo[c1]], axis=0).astype(BF16)
-        copies = (
-            remote(sendg.at[o], bgeo[o].at[pl.ds(core * 2, 2)], s_bg.at[o], r_bg.at[o], along(-o - 1)),
-            remote(sendd.at[o], bown[o], s_bd.at[o], r_bd.at[o], along(-o - 1)),
-        )
-        for copy in copies:
-            copy.start()
-        b_copies.append(copies)
-
+    loads[0].wait()
+    loads[1].wait()
     tops = [jnp.zeros((COLS, RANK), F32) for _ in range(TOPS)]
     for c in range(CL):
         leaf = mm_nt(den[:, c * PS : (c + 1) * PS], src_basis[c])
         child = mm_nt(leaf, up[c], HIGHEST)
         for t in range(TOPS):
             tops[t] = tops[t] + jnp.where(parent[c] == t, child, 0.0)
-    flat = (x * Y + y) * Z + z
     for h in range(2):
-        table[2 * flat + h] = jnp.concatenate(tops[4 * h : 4 * h + 4], axis=1).astype(BF16)
+        table[2 * me + h] = jnp.concatenate(tops[4 * h : 4 * h + 4], axis=1).astype(BF16)
 
     def gather_step(start, size, peers, send, recv):
         block = table.at[pl.ds(start, size)]
@@ -186,14 +221,37 @@
             copy.start()
         return copies
 
-    z_copies = gather_step(2 * flat, 2, z_peers, s_z, r_z)
+    y_copies = gather_step(2 * me, 2, y_peers, s_y, r_y)
+
+    b_copies = []
+    for o in range(W):
+        idx_copies[o].wait()
+        for m in range(CAP):
+            sendd[o, m] = dens[ridx[o][LIST + m]]
+        for m in range(2):
+            c0 = ridx[o][LIST + core * 4 + 2 * m]
+            c1 = ridx[o][LIST + core * 4 + 2 * m + 1]
+            sendg[o, m] = jnp.concatenate([geo[c0], geo[c1]], axis=0).astype(BF16)
+        half = pl.ds(core * 2, 2)
+        copies = (
+            remote(sendg.at[o], bgeo[o].at[half], s_bg.at[o], r_bg.at[o], along(-o - 1)),
+            remote(sendd.at[o], bown[o], s_bd.at[o], r_bd.at[o], along(-o - 1)),
+        )
+        b_copies.append(copies)
+        if o == 0:
+            for copy in copies:
+                copy.start()
 
     for t in range(HALF):
         left[t], right[t] = target_features(geo[mine + t])
+    for copy in b_copies[1]:
+        copy.start()
+    for copy in y_copies:
+        copy.wait()
+    z_copies = gather_step((x * Z + z) * Y * 2, Y * 2, z_peers, s_z, r_z)
     sib_copy.wait()
-    for copy in z_copies:
-        copy.wait()
-    y_copies = gather_step((x * Y + y) * Z * 2, Z * 2, y_peers, s_y, r_y)
+    for o in range(W):
+        name_targets(pairs, o, mine, idx[o], slots[o])
 
     def densities(t):
         own = den[:, pl.ds(pl.multiple_of((mine + t) * PS, PS), PS)]
@@ -209,7 +267,7 @@
 
     lax.fori_loop(0, HALF // 2, self_pair, 0)
 
-    for copy in y_copies:
+    for copy in z_copies:
         copy.wait()
     x_copies = gather_step(x * Y * Z * 2, Y * Z * 2, x_peers, s_x, r_x)
 
@@ -225,40 +283,61 @@
             copy.start()
         return forwards
 
-    def cross(o, forwards):
+    def prepare(o, forwards):
         for copy in forwards:
             copy.wait()
         for m in range(CAP):
             pair = bgeo[o][m // 2].astype(F32)
             bright[m] = source_features(pair[8 * (m % 2) : 8 * (m % 2) + 8])
-        live = jnp.where(me + o + 1 < N, 1.0, 0.0).astype(F32)
-
+
+    def cross(o, first, last, later):
         def cross_pair(u, carry):
             for k in range(2):
                 t = 2 * u + k
-                m = idx[o][SLOT + mine + t]
+                m = slots[o][t]
                 q = mm(left[t, :, 0:16], bright[m, 0:16])
                 nf = mm(left[t, :, 16:48], bright[m, 16:48])
                 nb = mm(left[t, :, 48:80], bright[m, 48:80])
                 scale = cube(q)
+                ybuf[t] = mm(densities(t), (nb * scale).astype(BF16))
+                if later:
+                    fbuf[t] = (nf * scale).astype(BF16)
+                else:
+                    there = jnp.concatenate([bown[o][m], bsib[o][m]], axis=0)
+                    near[t] += live(o) * mm_nt(there, (nf * scale).astype(BF16))
+            return carry
+
+        lax.fori_loop(first // 2, last // 2, cross_pair, 0)
+
+    def live(o):
+        return jnp.where(me + o + 1 < N, 1.0, 0.0).astype(F32)
+
+    def cross_rest(o):
+        def rest_pair(u, carry):
+            for k in range(2):
+                t = 2 * u + k
+                m = slots[o][t]
                 there = jnp.concatenate([bown[o][m], bsib[o][m]], axis=0)
-                near[t] += live * mm_nt(there, (nf * scale).astype(BF16))
-                ybuf[t] = mm(densities(t), (nb * scale).astype(BF16))
+                near[t] += live(o) * mm_nt(there, fbuf[t])
             return carry
 
-        lax.fori_loop(0, HALF // 2, cross_pair, 0)
-        for rows, dst in ((0, part_own), (COLS, part_sib)):
+        lax.fori_loop(0, HALF // 2, rest_pair, 0)
+
+    def share(o):
+        copy = None
+        for rows, dst in ((COLS, part_sib), (0, part_own)):
             for r in range(0, COLS, 8):
                 tiles = [ybuf[t, rows + r : rows + r + 8, :] for t in range(HALF)]
                 for m in range(CAP):
                     total = None
                     for t in range(HALF):
-                        hit = jnp.where(idx[o][SLOT + mine + t] == m, 1.0, 0.0).astype(F32)
+                        hit = jnp.where(slots[o][t] == m, 1.0, 0.0).astype(F32)
                         term = hit * tiles[t]
                         total = term if total is None else total + term
                     dst[o, m, r : r + 8, :] = total
-        copy = remote(part_sib.at[o], part_recv.at[o], s_ps.at[o], r_ps.at[o], sibling)
-        copy.start()
+            if copy is None:
+                copy = remote(part_sib.at[o], part_recv.at[o], s_ps.at[o], r_ps.at[o], sibling)
+                copy.start()
         return copy
 
     def send_back(o, copy):
@@ -269,25 +348,33 @@
         back.start()
         return back
 
-    forwards = arrived(0)
-    part = cross(0, forwards)
+    prepare(0, arrived(0))
+    cross(0, 0, 4, False)
     forwards = arrived(1)
+    cross(0, 4, 8, False)
+    part = share(0)
+    prepare(1, forwards)
+    cross(1, 0, 4, True)
     backs = [send_back(0, part)]
-    part = cross(1, forwards)
+    cross(1, 4, 8, True)
+    part = share(1)
+    cross_rest(1)
+    backs.append(send_back(1, part))
     for t in range(HALF):
         near_sib[t] = near[t, COLS:, :]
     near_copy = remote(near_sib, near_recv, s_nr, r_nr, sibling)
     near_copy.start()
-    backs.append(send_back(1, part))
-
+
+    for load in loads[2:]:
+        load.wait()
     for copy in x_copies:
         copy.wait()
     lane = lax.broadcasted_iota(jnp.int32, (COLS, 128), 1) // RANK
     for t in range(TOPS):
         for f in range(FAR):
-            code = far_idx[t * FAR + f]
-            tile = table[code >> 2].astype(F32)
-            folded[t * FAR + f] = jnp.where(lane == (code & 3), tile, 0.0).astype(BF16)
+            top = far_src[t, f]
+            tile = table[top >> 2].astype(F32)
+            folded[t * FAR + f] = jnp.where(lane == (top & 3), tile, 0.0).astype(BF16)
     ones_row = lax.rem(lax.broadcasted_iota(jnp.int32, (128, 128), 0), RANK)
     ones_col = lax.rem(lax.broadcasted_iota(jnp.int32, (128, 128), 1), RANK)
     spread = jnp.where(ones_row == ones_col, 1.0, 0.0).astype(BF16)
@@ -327,21 +414,6 @@
             out[:, at] += keep * given
 
 
-def index_table(targets, sources):
-    slots = jnp.arange(CL, dtype=jnp.int32)
-    present = jnp.any(sources[None, :] == slots[:, None], axis=1).astype(jnp.int32)
-    rank = jnp.sum(jnp.where(slots[None, :] < slots[:, None], present[None, :], 0), axis=1)
-    place = (rank[None, :] == jnp.arange(CAP)[:, None]) & (present[None, :] == 1)
-    listed = jnp.sum(jnp.where(place, slots[None, :], 0), axis=1)
-    named = jnp.sum(
-        jnp.where(targets[None, :] == slots[:, None], sources[None, :], 0), axis=1
-    )
-    slot = jnp.sum(jnp.where(named[:, None] == slots[None, :], rank[None, :], 0), axis=1)
-    rank = jnp.minimum(rank, CAP - 1) * present
-    pad = jnp.zeros((128 - 56,), jnp.int32)
-    return jnp.concatenate([listed, slot, rank, present, pad]).astype(jnp.int32)
-
-
 def local(
     centers,
     normals,
@@ -356,20 +428,22 @@
     downward_transfer,
     tgt_basis,
 ):
-    tables = [index_table(near_pairs[0, o], near_pairs[1, o]) for o in range(W)]
-    dev, lane = far_src // TOPS, far_src % TOPS
-    place = ((dev // (Y * Z)) * Y + dev % Y) * Z + (dev // Y) % Z
-    far_idx = ((place * 2 + lane // 4) * 4 + lane % 4).reshape(-1).astype(jnp.int32)
-
     vmem = pl.BlockSpec(memory_space=pltpu.VMEM)
     smem = pl.BlockSpec(memory_space=pltpu.SMEM)
     dma = pltpu.SemaphoreType.DMA
     return pl.pallas_call(
         kernel,
         out_shape=jax.ShapeDtypeStruct((COLS, CL * PS), F32),
-        in_specs=[vmem] * 4 + [smem] * 4 + [vmem] * 5,
+        in_specs=[vmem] * 4 + [smem] * 3 + [pl.BlockSpec(memory_space=pl.ANY)] * 5,
         out_specs=vmem,
         scratch_shapes=[
+            pltpu.VMEM((CL, RANK, PS), BF16),
+            pltpu.VMEM((CL, RANK, RANK), F32),
+            pltpu.VMEM((TOPS * RANK, FAR * RANK), BF16),
+            pltpu.VMEM((CL, RANK, RANK), F32),
+            pltpu.VMEM((CL, RANK, PS), BF16),
+            dma((5,)),
+            pltpu.SMEM((64,), jnp.int32),
             pltpu.VMEM((CL, 8, PS), F32),
             pltpu.VMEM((CL, COLS, PS), BF16),
             pltpu.VMEM((HALF, PS, 128), BF16),
@@ -386,6 +460,7 @@
             pltpu.VMEM((CAP, 80, PS), BF16),
             pltpu.VMEM((HALF, 2 * COLS, PS), F32),
             pltpu.VMEM((HALF, 2 * COLS, PS), F32),
+            pltpu.VMEM((HALF, PS, PS), BF16),
             pltpu.VMEM((W, CAP, COLS, PS), F32),
             pltpu.VMEM((W, CAP, COLS, PS), F32),
             pltpu.VMEM((W, CAP, COLS, PS), F32),
@@ -399,6 +474,10 @@
             pltpu.VMEM((TOPS, COLS, RANK), F32),
             pltpu.SMEM((128,), jnp.int32),
             pltpu.SMEM((128,), jnp.int32),
+            pltpu.SMEM((128,), jnp.int32),
+            pltpu.SMEM((128,), jnp.int32),
+            pltpu.SMEM((HALF,), jnp.int32),
+            pltpu.SMEM((HALF,), jnp.int32),
             dma((W,)), dma((W,)),
             dma, dma,
             dma((W,)), dma((W,)),
@@ -420,9 +499,9 @@
         normals,
         weights.reshape(1, -1),
         density,
-        *tables,
+        near_pairs,
         parent,
-        far_idx,
+        far_src,
         src_basis,
         upward_transfer,
         far_mat.reshape(TOPS * RANK, FAR * RANK),

time: 62.8 us -> 53.5 us (0.85)
  Pallas kernels: 56.2 us -> 50.1 us
  local copies, waits for them, and re-layouts: 5.21 us -> 3.22 us
  other arithmetic: 1.11 us -> 0 us
    pallas_call x1, Pallas kernels: 56.2 us -> 50.1 us  [local(): pl.pallas_call(kernel, out_shape=jax.ShapeDtypeStruct((COLS, CL * PS), F3...]
    concatenate x2 -> x0, local copies, waits for them, and re-layouts: 1.26 us -> none  [index_table(): return jnp.concatenate([listed, slot, rank, present, pad]).astype(jnp.int32)]
    reduce_sum x7 -> x0, other arithmetic: 0.94 us -> none  [the longest x2 0.36 us: index_table(): jnp.sum(jnp.where(named[:, None] == slots[None, :], rank[None, :], 0), ax...]
    eq x1 -> x0, local copies, waits for them, and re-layouts: 0.76 us -> none  [index_table(): targets[None, :] == slots[:, None]]
    reshape x1, local copies, waits for them, and re-layouts: 0.63 us -> 1.35 us  [local(): weights.reshape(1, -1)]
    reshape x1 -> x0, local copies, waits for them, and re-layouts: 0.67 us -> none  [local(): ((place * 2 + lane // 4) * 4 + lane % 4).reshape(-1).astype(jnp.int32)]
    unnamed x5 -> x1, local copies, waits for them, and re-layouts: 1.88 us -> 1.87 us
where the time goes in v2:
time: 53.5 us; the launch traced here: 53.3 us
  Pallas kernels  50.1 us (94%)
  local copies, waits for them, and re-layouts  3.22 us (6%)
    pallas_call x1, Pallas kernels, local(): pl.pallas_call(kernel, out_shape=jax.ShapeDtypeStruct((COLS, CL * PS), F3...  50.1 us
    unnamed x1, local copies, waits for them, and re-layouts  1.87 us
    reshape x1, local copies, waits for them, and re-layouts, local(): weights.reshape(1, -1)  1.35 us

profile of v2, /device:TPU:1, one launch (start us, length us, event | category | flops | bytes accessed | tf_op | source)
XLA Modules:
  0.0 53.3 jit_solution(10537794383412744252)
XLA Ops:
  0.0 1.3 %reshape.6.wts = bf16[1,8192]{1,0:T(2,128)(2,1)} reshape(bf16[8192]{0:T(1024)(128)(2,1)} %param.14) | data formatting | bytes 32768 | tf_op jit(solution)/shard_map/reshape | solution.py:500
  1.4 50.1 %shard_map.118 = f32[16,8192]{1,0:T(8,128)} custom-call(bf16[3,8192]{1,0:T(4,128)(2,1)} %cen.1, bf16[3,8192]{1,0:T(4,128)(2,1)} %nor.1, bf16[1,8192]{1,0:T(2,128)(2,1)} %reshape.6.wts, bf16[16,8192]{1,0:T(8,128)(2,1)} %den.1, s32[2,2,16]{2,1,0:T(2,128)} %pairs.1, s32[16]{0:T(128)} %parent.1, s32[8,32]{1,0:T(8,128)} %far_src.1, ...), custom_call_target="tpu_custom_call" | custom-call | tf_op jit(solution)/shard_map/pallas_call | solution.py:434
  51.5 1.9 %copy.14 = f32[16,8192]{1,0:T(8,128)} copy(f32[16,8192]{1,0:T(8,128)} %shard_map.118) | data formatting | bytes 1048576

commit v3 on v2

--- a/solution.py
+++ b/solution.py
@@ -143,6 +143,15 @@
     ret_recv = (ret_recv1, ret_recv2)
     mine = core * HALF
     other = (1 - core) * HALF
+
+    ahead = [me + o + 1 < N for o in range(W)]
+    behind = [me - o - 1 >= 0 for o in range(W)]
+
+    def when(condition, *steps):
+        @pl.when(condition)
+        def _():
+            for step in steps:
+                step()
 
     def along(step):
         return {"clus": lax.rem(me + step + N, N)}
@@ -188,8 +197,8 @@
     idx_copies = [
         remote(idx[o], ridx[o], s_idx.at[o], r_idx.at[o], along(o + 1)) for o in range(W)
     ]
-    for copy in idx_copies:
-        copy.start()
+    for o in range(W):
+        when(ahead[o], idx_copies[o].start)
     sib_copy = remote(
         den.at[:, pl.ds(pl.multiple_of(other * PS, PS), HALF * PS)], dsib, s_sib, r_sib, sibling
     )
@@ -197,16 +206,22 @@
 
     for c in range(CL):
         at = pl.ds(c * PS, PS)
-        rows = [cen[:, at].astype(F32), nor[:, at].astype(F32), wts[:, at].astype(F32)]
+        w = wts[at].astype(F32).reshape(1, PS)
+        rows = [cen[:, at].astype(F32), nor[:, at].astype(F32), w]
         dens[c] = den[:, at]
         geo[c] = jnp.concatenate(rows + [jnp.zeros((1, PS), F32)], axis=0)
 
     loads[0].wait()
     loads[1].wait()
+    def blocks(wide):
+        return [
+            wide[c * COLS : (c + 1) * COLS, c * RANK : (c + 1) * RANK] for c in range(CL)
+        ]
+
+    leaf = mm_nt(dens[...].reshape(CL * COLS, PS), src_basis[...].reshape(CL * RANK, PS))
+    leaf = jnp.concatenate(blocks(leaf), axis=0)
     tops = [jnp.zeros((COLS, RANK), F32) for _ in range(TOPS)]
-    for c in range(CL):
-        leaf = mm_nt(den[:, c * PS : (c + 1) * PS], src_basis[c])
-        child = mm_nt(leaf, up[c], HIGHEST)
+    for c, child in enumerate(blocks(mm_nt(leaf, up[...].reshape(CL * RANK, RANK), HIGHEST))):
         for t in range(TOPS):
             tops[t] = tops[t] + jnp.where(parent[c] == t, child, 0.0)
     for h in range(2):
@@ -225,27 +240,34 @@
 
     b_copies = []
     for o in range(W):
-        idx_copies[o].wait()
-        for m in range(CAP):
-            sendd[o, m] = dens[ridx[o][LIST + m]]
-        for m in range(2):
-            c0 = ridx[o][LIST + core * 4 + 2 * m]
-            c1 = ridx[o][LIST + core * 4 + 2 * m + 1]
-            sendg[o, m] = jnp.concatenate([geo[c0], geo[c1]], axis=0).astype(BF16)
+
+        def gather(o=o):
+            idx_copies[o].wait_recv()
+            for m in range(CAP):
+                sendd[o, m] = dens[ridx[o][LIST + m]]
+            for m in range(2):
+                c0 = ridx[o][LIST + core * 4 + 2 * m]
+                c1 = ridx[o][LIST + core * 4 + 2 * m + 1]
+                sendg[o, m] = jnp.concatenate([geo[c0], geo[c1]], axis=0).astype(BF16)
+
+        when(behind[o], gather)
         half = pl.ds(core * 2, 2)
         copies = (
             remote(sendg.at[o], bgeo[o].at[half], s_bg.at[o], r_bg.at[o], along(-o - 1)),
-            remote(sendd.at[o], bown[o], s_bd.at[o], r_bd.at[o], along(-o - 1)),
+            *(
+                remote(
+                    sendd.at[o, pl.ds(4 * h, 4)], bown[o].at[pl.ds(4 * h, 4)],
+                    s_bd.at[o, h], r_bd.at[o, h], along(-o - 1),
+                )
+                for h in range(2)
+            ),
         )
         b_copies.append(copies)
         if o == 0:
-            for copy in copies:
-                copy.start()
+            when(behind[o], *(copy.start for copy in copies))
 
     for t in range(HALF):
         left[t], right[t] = target_features(geo[mine + t])
-    for copy in b_copies[1]:
-        copy.start()
     for copy in y_copies:
         copy.wait()
     z_copies = gather_step((x * Z + z) * Y * 2, Y * 2, z_peers, s_z, r_z)
@@ -265,27 +287,33 @@
             near[t] = mm(densities(t), (nb * cube(q)).astype(BF16))
         return carry
 
-    lax.fori_loop(0, HALF // 2, self_pair, 0)
-
+    lax.fori_loop(0, HALF // 4, self_pair, 0)
+
+    when(behind[1], *(copy.start for copy in b_copies[1]))
     for copy in z_copies:
         copy.wait()
     x_copies = gather_step(x * Y * Z * 2, Y * Z * 2, x_peers, s_x, r_x)
 
     def arrived(o):
-        for copy in b_copies[o]:
-            copy.wait()
         half = pl.ds(core * 2, 2)
-        forwards = (
-            remote(bgeo[o].at[half], bgeo[o].at[half], s_fg.at[o], r_fg.at[o], sibling),
-            remote(bown[o], bsib[o], s_fd.at[o], r_fd.at[o], sibling),
-        )
-        for copy in forwards:
-            copy.start()
+        forwards = [remote(bgeo[o].at[half], bgeo[o].at[half], s_fg.at[o], r_fg.at[o], sibling)]
+        for h in range(2):
+            part = pl.ds(4 * h, 4)
+            forwards.append(
+                remote(bown[o].at[part], bsib[o].at[part], s_fd.at[o, h], r_fd.at[o, h], sibling)
+            )
+
+        def pass_on():
+            for arrival, forward in zip(b_copies[o], forwards):
+                arrival.wait_recv()
+                forward.start()
+
+        when(ahead[o], pass_on)
+        when(behind[o], *(copy.wait_send for copy in b_copies[o]))
         return forwards
 
     def prepare(o, forwards):
-        for copy in forwards:
-            copy.wait()
+        when(ahead[o], *(copy.wait for copy in forwards))
         for m in range(CAP):
             pair = bgeo[o][m // 2].astype(F32)
             bright[m] = source_features(pair[8 * (m % 2) : 8 * (m % 2) + 8])
@@ -304,13 +332,11 @@
                     fbuf[t] = (nf * scale).astype(BF16)
                 else:
                     there = jnp.concatenate([bown[o][m], bsib[o][m]], axis=0)
-                    near[t] += live(o) * mm_nt(there, (nf * scale).astype(BF16))
+                    there = mm_nt(there, (nf * scale).astype(BF16))
+                    near[t] += jnp.where(ahead[o], there, 0.0)
             return carry
 
         lax.fori_loop(first // 2, last // 2, cross_pair, 0)
-
-    def live(o):
-        return jnp.where(me + o + 1 < N, 1.0, 0.0).astype(F32)
 
     def cross_rest(o):
         def rest_pair(u, carry):
@@ -318,37 +344,54 @@
                 t = 2 * u + k
                 m = slots[o][t]
                 there = jnp.concatenate([bown[o][m], bsib[o][m]], axis=0)
-                near[t] += live(o) * mm_nt(there, fbuf[t])
+                near[t] += jnp.where(ahead[o], mm_nt(there, fbuf[t]), 0.0)
             return carry
 
         lax.fori_loop(0, HALF // 2, rest_pair, 0)
 
     def share(o):
-        copy = None
-        for rows, dst in ((COLS, part_sib), (0, part_own)):
-            for r in range(0, COLS, 8):
-                tiles = [ybuf[t, rows + r : rows + r + 8, :] for t in range(HALF)]
-                for m in range(CAP):
-                    total = None
-                    for t in range(HALF):
-                        hit = jnp.where(slots[o][t] == m, 1.0, 0.0).astype(F32)
-                        term = hit * tiles[t]
-                        total = term if total is None else total + term
-                    dst[o, m, r : r + 8, :] = total
-            if copy is None:
-                copy = remote(part_sib.at[o], part_recv.at[o], s_ps.at[o], r_ps.at[o], sibling)
-                copy.start()
-        return copy
-
-    def send_back(o, copy):
-        copy.wait()
-        for m in range(CAP):
-            ret_send[o, m] = (part_own[o, m] + part_recv[o, m]).astype(BF16)
-        back = remote(ret_send.at[o], ret_recv[o], s_rt.at[o], r_rt.at[o], along(o + 1))
-        back.start()
-        return back
-
-    prepare(0, arrived(0))
+        copies = []
+        for h in range(2):
+            for rows, dst in ((COLS, part_sib), (0, part_own)):
+                for r in range(0, COLS, 8):
+                    tiles = [ybuf[t, rows + r : rows + r + 8, :] for t in range(HALF)]
+                    for m in range(4 * h, 4 * h + 4):
+                        total = None
+                        for t in range(HALF):
+                            hit = jnp.where(slots[o][t] == m, 1.0, 0.0).astype(F32)
+                            term = hit * tiles[t]
+                            total = term if total is None else total + term
+                        dst[o, m, r : r + 8, :] = total
+                if rows == COLS:
+                    part = pl.ds(4 * h, 4)
+                    copies.append(
+                        remote(
+                            part_sib.at[o, part], part_recv.at[o, part],
+                            s_ps.at[o, h], r_ps.at[o, h], sibling,
+                        )
+                    )
+                    copies[-1].start()
+        return copies
+
+    def send_back(o, copies):
+        returned = []
+        for h in range(2):
+            copies[h].wait()
+            for m in range(4 * h, 4 * h + 4):
+                ret_send[o, m] = (part_own[o, m] + part_recv[o, m]).astype(BF16)
+            part = pl.ds(4 * h, 4)
+            returned.append(
+                remote(
+                    ret_send.at[o, part], ret_recv[o].at[part],
+                    s_rt.at[o, h], r_rt.at[o, h], along(o + 1),
+                )
+            )
+            when(ahead[o], returned[-1].start)
+        return returned
+
+    forwards = arrived(0)
+    lax.fori_loop(HALF // 4, HALF // 2, self_pair, 0)
+    prepare(0, forwards)
     cross(0, 0, 4, False)
     forwards = arrived(1)
     cross(0, 4, 8, False)
@@ -394,9 +437,15 @@
     distant = mm_nt(jnp.concatenate(picked, axis=0), far_mat[...])
     for t in range(TOPS):
         far_top[t] = distant[t * COLS : (t + 1) * COLS, t * RANK : (t + 1) * RANK]
+    upper = jnp.concatenate([far_top[parent[c]] for c in range(CL)], axis=0)
+    lower = mm_nt(upper, down[...].reshape(CL * RANK, RANK), HIGHEST)
+    same = lax.broadcasted_iota(jnp.int32, lower.shape, 0) // COLS == (
+        lax.broadcasted_iota(jnp.int32, lower.shape, 1) // RANK
+    )
+    lower = jnp.where(same, lower, 0.0).astype(BF16)
+    far_part = mm(lower, tgt_basis[...].reshape(CL * RANK, PS))
     for c in range(CL):
-        lower = mm_nt(far_top[parent[c]], down[c], HIGHEST).astype(BF16)
-        out[:, c * PS : (c + 1) * PS] = mm(lower, tgt_basis[c])
+        out[:, c * PS : (c + 1) * PS] = far_part[c * COLS : (c + 1) * COLS]
 
     near_copy.wait()
     for t in range(HALF):
@@ -405,13 +454,17 @@
         at = pl.ds(pl.multiple_of((other + t) * PS, PS), PS)
         out[:, at] += near_recv[t]
     for o in range(W):
-        backs[o].wait()
-        behind = jnp.where(me - o - 1 >= 0, 1.0, 0.0).astype(F32)
-        for c in range(CL):
-            at = pl.ds(c * PS, PS)
-            given = ret_recv[o][ridx[o][RANKED + c]].astype(F32)
-            keep = behind * ridx[o][PRESENT + c].astype(F32)
-            out[:, at] += keep * given
+        when(ahead[o], idx_copies[o].wait_send, *(copy.wait_send for copy in backs[o]))
+
+        def add(o=o):
+            for copy in backs[o]:
+                copy.wait_recv()
+            for c in range(CL):
+                at = pl.ds(c * PS, PS)
+                given = ret_recv[o][ridx[o][RANKED + c]].astype(F32)
+                out[:, at] += ridx[o][PRESENT + c].astype(F32) * given
+
+        when(behind[o], add)
 
 
 def local(
@@ -480,12 +533,12 @@
             pltpu.SMEM((HALF,), jnp.int32),
             dma((W,)), dma((W,)),
             dma, dma,
+            dma((W, 2)), dma((W, 2)),
             dma((W,)), dma((W,)),
+            dma((W, 2)), dma((W, 2)),
             dma((W,)), dma((W,)),
-            dma((W,)), dma((W,)),
-            dma((W,)), dma((W,)),
-            dma((W,)), dma((W,)),
-            dma((W,)), dma((W,)),
+            dma((W, 2)), dma((W, 2)),
+            dma((W, 2)), dma((W, 2)),
             dma, dma,
             dma((Z - 1,)), dma((Z - 1,)),
             dma((Y - 1,)), dma((Y - 1,)),
@@ -497,7 +550,7 @@
     )(
         centers,
         normals,
-        weights.reshape(1, -1),
+        weights,
         density,
         near_pairs,
         parent,

time: 53.5 us -> 50 us (0.935)
  the two profiles are of different devices: /device:TPU:1 before, /device:TPU:2 now
where the time goes in v3:
time: 50 us; the launch traced here: 49.9 us
  Pallas kernels  48 us (96%)
  local copies, waits for them, and re-layouts  1.87 us (4%)
    pallas_call x1, Pallas kernels, local(): pl.pallas_call(kernel, out_shape=jax.ShapeDtypeStruct((COLS, CL * PS), F3...  48 us
    unnamed x1, local copies, waits for them, and re-layouts  1.87 us

profile of v3, /device:TPU:2, one launch (start us, length us, event | category | flops | bytes accessed | tf_op | source)
XLA Modules:
  0.0 49.9 jit_solution(12885284793435086480)
XLA Ops:
  0.0 48.0 %shard_map.118 = f32[16,8192]{1,0:T(8,128)} custom-call(bf16[3,8192]{1,0:T(4,128)(2,1)} %cen.1, bf16[3,8192]{1,0:T(4,128)(2,1)} %nor.1, bf16[8192]{0:T(1024)(128)(2,1)} %wts.1, bf16[16,8192]{1,0:T(8,128)(2,1)} %den.1, s32[2,2,16]{2,1,0:T(2,128)} %pairs.1, s32[16]{0:T(128)} %parent.1, s32[8,32]{1,0:T(8,128)} %far_src.1, bf16[16,32,512]{2,1,0:T(8,128)(2,1)} %src_basis_hbm.1, ...), custom_call_target="tpu_custom_call" | custom-call | tf_op jit(solution)/shard_map/pallas_call | solution.py:487
  48.0 1.9 %copy.14 = f32[16,8192]{1,0:T(8,128)} copy(f32[16,8192]{1,0:T(8,128)} %shard_map.118) | data formatting | bytes 1048576

commit v4 on v3

--- a/solution.py
+++ b/solution.py
@@ -320,8 +320,8 @@
 
     def cross(o, first, last, later):
         def cross_pair(u, carry):
-            for k in range(2):
-                t = 2 * u + k
+            for k in range(4):
+                t = 4 * u + k
                 m = slots[o][t]
                 q = mm(left[t, :, 0:16], bright[m, 0:16])
                 nf = mm(left[t, :, 16:48], bright[m, 16:48])
@@ -336,7 +336,7 @@
                     near[t] += jnp.where(ahead[o], there, 0.0)
             return carry
 
-        lax.fori_loop(first // 2, last // 2, cross_pair, 0)
+        lax.fori_loop(first // 4, last // 4, cross_pair, 0)
 
     def cross_rest(o):
         def rest_pair(u, carry):

time: 50 us -> 49.5 us (0.990)
  Pallas kernels: 48 us -> 47.5 us
    pallas_call x1, Pallas kernels: 48 us -> 47.5 us  [local(): pl.pallas_call(kernel, out_shape=jax.ShapeDtypeStruct((COLS, CL * PS), F3...]
where the time goes in v4:
time: 49.5 us; the launch traced here: 49.3 us
  Pallas kernels  47.5 us (96%)
  local copies, waits for them, and re-layouts  1.87 us (4%)
    pallas_call x1, Pallas kernels, local(): pl.pallas_call(kernel, out_shape=jax.ShapeDtypeStruct((COLS, CL * PS), F3...  47.5 us
    unnamed x1, local copies, waits for them, and re-layouts  1.87 us

profile of v4, /device:TPU:2, one launch (start us, length us, event | category | flops | bytes accessed | tf_op | source)
XLA Modules:
  0.0 49.3 jit_solution(14868175627370068989)
XLA Ops:
  0.0 47.5 %shard_map.118 = f32[16,8192]{1,0:T(8,128)} custom-call(bf16[3,8192]{1,0:T(4,128)(2,1)} %cen.1, bf16[3,8192]{1,0:T(4,128)(2,1)} %nor.1, bf16[8192]{0:T(1024)(128)(2,1)} %wts.1, bf16[16,8192]{1,0:T(8,128)(2,1)} %den.1, s32[2,2,16]{2,1,0:T(2,128)} %pairs.1, s32[16]{0:T(128)} %parent.1, s32[8,32]{1,0:T(8,128)} %far_src.1, bf16[16,32,512]{2,1,0:T(8,128)(2,1)} %src_basis_hbm.1, ...), custom_call_target="tpu_custom_call" | custom-call | tf_op jit(solution)/shard_map/pallas_call | solution.py:487
  47.5 1.9 %copy.14 = f32[16,8192]{1,0:T(8,128)} copy(f32[16,8192]{1,0:T(8,128)} %shard_map.118) | data formatting | bytes 1048576
